TPU v7x, 256 devices: a whole 4x4x8 slice. The times are simulated.
256 devices in a mesh: lat: 8 (over x, y_lo), lon: 32 (over y_hi, z, core).
Axes of the slice: x: 4, y: 4 (y_hi: 2, y_lo: 2; y = y_hi * 2 + y_lo), z: 8, core: 2. Of those that a mesh axis runs over, the one named last changes fastest.
Arguments:
- tracers: float32 [2, 12, 128, 4096], P(None, None, 'lat', 'lon'), may hold values from -6 to 6
- wet_levels: int32 [128, 4096], P('lat', 'lon'), may hold values from 0 to 12, as said below
- east_speed: float32 [12, 128, 4096], P(None, 'lat', 'lon'), may hold values from -0.25 to 0.25
- north_speed: float32 [12, 128, 4096], P(None, 'lat', 'lon'), may hold values from -0.25 to 0.25
- down_speed: float32 [12, 128, 4096], P(None, 'lat', 'lon'), may hold values from -0.25 to 0.25
- east_diffusivity: float32 [12, 128, 4096], P(None, 'lat', 'lon'), may hold values from 0.02 to 0.12
- east_slope: float32 [12, 128, 4096], P(None, 'lat', 'lon'), may hold values from -1 to 1
- north_diffusivity: float32 [12, 128, 4096], P(None, 'lat', 'lon'), may hold values from 0.02 to 0.12
- north_slope: float32 [12, 128, 4096], P(None, 'lat', 'lon'), may hold values from -1 to 1
- down_diffusivity: float32 [12, 128, 4096], P(None, 'lat', 'lon'), may hold values from 0.02 to 0.12
- down_slope_east: float32 [12, 128, 4096], P(None, 'lat', 'lon'), may hold values from -1 to 1
- down_slope_north: float32 [12, 128, 4096], P(None, 'lat', 'lon'), may hold values from -1 to 1
Outputs:
- evolved_tracers: float32 [2, 12, 128, 4096], P(None, None, 'lat', 'lon')
Inputs may be any that keep to these rules, and one draw needn't show every extreme that they name: `wet_levels`: 0 marks a land column. Land comes as single columns, as aligned blocks of 8 x 8 columns and as whole aligned blocks of 16 x 128 columns.
All inputs are finite; a program needn't handle non-finite values.
Results may differ from a plain program's by a relative error of at most 0.0003.
Values sent between devices are 32-bit elements; how exact they have to be, the bound alone decides.
No kernel may reach another device: no remote copies, remote signals or barrier semaphores. Data moves between devices by JAX's collectives and lax.ppermute only.
A program may use at most 64 MiB of HBM per device.

v0:
```python
import jax
import jax.numpy as jnp
from jax import lax
from jax.experimental import pallas as pl
from jax.experimental.pallas import tpu as pltpu
from jax.sharding import PartitionSpec as P

STEPS = 3
K = 12
ROWS = 16
LANES = 128
EXT = 32
PAD = 48
NORTHWARD = (3, 4, 5)
EASTWARD = (0, 1, 2)
FLIPPED = (0, 2, 3, 5, 8, 9)
STATICS = 10
SLOTS = 19
VMEM_LIMIT = 48 * 1024 * 1024
FULL = 63 * 1024 * 1024


def lane_roll(x, shift):
    return pltpu.roll(x, shift % x.shape[-1], x.ndim - 1)


def row_roll(x, shift):
    return pltpu.roll(x, shift % x.shape[0], 0)


def lanes_of(shape):
    return lax.broadcasted_iota(jnp.int32, shape, len(shape) - 1)


def is_even(axis):
    return lax.rem(lax.axis_index(axis), 2) == 0


def is_top():
    return lax.axis_index("lat") == lax.axis_size("lat") - 1


def pack_band(dst, tracers, levels, statics, northward):
    low4 = ROWS - 4 if northward else 0
    low6 = ROWS - 6 if northward else 0
    extra = ROWS - 5 if northward else 0
    for k in range(K):
        for f in range(STATICS):
            dst[k, 4 * f : 4 * f + 4, :] = statics[f][k, low4 : low4 + 4, :]
        for t in range(2):
            dst[k, 40 + 6 * t : 46 + 6 * t, :] = tracers[t, k, low6 : low6 + 6, :]
        for n, f in enumerate(NORTHWARD):
            dst[k, 52 + n : 53 + n, :] = statics[f][k, extra : extra + 1, :]
        row = low6 + k if k < 6 else 0
        dst[k, 55:56, :] = levels[row : row + 1, :].astype(jnp.float32)


def band_kernel(tracers, levels, *refs):
    statics, (_, near, far) = refs[:STATICS], refs[STATICS:]
    even = is_even("lat")

    @pl.when(even)
    def _():
        pack_band(near, tracers, levels, statics, True)
        pack_band(far, tracers, levels, statics, False)

    @pl.when(jnp.logical_not(even))
    def _():
        pack_band(far, tracers, levels, statics, True)
        pack_band(near, tracers, levels, statics, False)


def side_kernel(tracers, levels, *refs):
    statics, (sides,) = refs[:STATICS], refs[STATICS:]
    place = lanes_of((8, LANES)) // 16
    for tile in range(2):
        rows = slice(8 * tile, 8 * tile + 8)
        for v in range(SLOTS):
            packed = jnp.zeros((8, LANES), jnp.float32)
            for q in range(8):
                slot = 8 * v + q
                f, k = slot // K, slot % K
                if slot == 12 * K:
                    value = levels[rows, :].astype(jnp.float32)
                elif slot > 12 * K:
                    continue
                elif f < STATICS:
                    value = statics[f][k, rows, :]
                else:
                    value = tracers[f - STATICS, k, rows, :]
                packed = jnp.where(place == q, lane_roll(value, 8 + 16 * q), packed)
            sides[tile, v] = packed


def corner_kernel(near_side, far_side, merged, near, far):
    even_lon, even_lat = is_even("lon"), is_even("lat")
    low = lanes_of((8, LANES)) % 16 < 8
    for tile in range(2):
        for v in range(SLOTS):
            a, b = near_side[tile, v], far_side[tile, v]
            east = jnp.where(even_lon, a, b)
            west = jnp.where(even_lon, b, a)
            merged[tile, v] = jnp.where(low, lane_roll(east, -8), lane_roll(west, 8))
    for v in range(SLOTS):
        bottom, top = merged[0, v], merged[1, v]
        near[v] = jnp.where(even_lat, top, bottom)
        far[v] = jnp.where(even_lat, bottom, top)


def minmod(p, q):
    return jnp.maximum(jnp.minimum(p, q), 0.0) + jnp.minimum(jnp.maximum(p, q), 0.0)


def signed_half(c):
    return jnp.where(c > 0, 0.5, -0.5) - 0.5 * c


def face_flux(c, h, spread, tilt, here, there, before, jump, after, grads):
    up = c > 0
    slope = minmod(jnp.where(up, before, after), jump)
    return c * (jnp.where(up, here, there) + h * slope) - spread * (jump + tilt * grads)


def at(tile, shift=0):
    return slice(8 + 8 * tile + shift, 16 + 8 * tile + shift)


def plain(tile):
    return slice(8 * tile, 8 * tile + 8)


def level_tables(level, table):
    table[0, 8 : 8 + EXT, :] = level
    table[1, 8 : 8 + EXT, :] = jnp.minimum(level, lane_roll(level, -1))
    table[2, 8 : 8 + EXT, :] = jnp.minimum(level, row_roll(level, -1))


def derive(raw, put, seam_raw, seam_put, table):
    for tile in range(4):
        rows = plain(tile)
        level, east_level, north_level = (table[i, at(tile), :] for i in range(3))
        for k in range(K):
            east, north, lower = east_level > k, north_level > k, level > k + 1
            c = raw[0, k, rows, :]
            put[0, k, rows, :] = jnp.where(east, c, 0.0)
            put[1, k, rows, :] = signed_half(c)
            put[2, k, rows, :] = raw[1, k, rows, :]
            put[3, k, rows, :] = jnp.where(east, 0.25 * raw[2, k, rows, :], 0.0)
            c = raw[3, k, rows, :]
            put[4, k, rows, :] = jnp.where(north, c, 0.0)
            put[5, k, rows, :] = signed_half(c)
            put[6, k, rows, :] = raw[4, k, rows, :]
            put[7, k, rows, :] = jnp.where(north, 0.25 * raw[5, k, rows, :], 0.0)
            if tile == 2:
                c = seam_raw[0, k]
                seam_put[0, k] = jnp.where(north, c, 0.0)
                seam_put[1, k] = signed_half(c)
                seam_put[2, k] = seam_raw[1, k]
                seam_put[3, k] = jnp.where(north, 0.25 * seam_raw[2, k], 0.0)
            if k < K - 1:
                c, spread = raw[6, k, rows, :], raw[7, k, rows, :]
                along, across = raw[8, k, rows, :], raw[9, k, rows, :]
                put[8, k, rows, :] = jnp.where(lower, c, 0.0)
                put[9, k, rows, :] = signed_half(c)
                put[10, k, rows, :] = spread * (along * along + across * across)
                masked = jnp.where(lower, 0.25 * spread, 0.0)
                put[11, k, rows, :] = masked * along
                put[12, k, rows, :] = masked * across


def grads_pass(x, doms, table, dz, tz):
    for tile in range(4):
        level = table[0, at(tile), :]
        for dom in doms:
            above = None
            here = x[dom, 0, at(tile), :]
            for k in range(K):
                if k < K - 1:
                    below = x[dom, k + 1, at(tile), :]
                    d = jnp.where(level > k + 1, below - here, 0.0)
                    dz[dom, k, plain(tile), :] = d
                    tz[dom, k, at(tile), :] = d if above is None else above + d
                    here, above = below, d
                else:
                    tz[dom, k, at(tile), :] = above


def sides_pass(x, doms, table, statics, seam, tz, fx, fy, tx, ty, fseam, tiles):
    for tile in range(4):
        if tile not in tiles and tile + 1 not in tiles:
            continue
        east = table[1, at(tile), :]
        east_m, east_1 = lane_roll(east, 1), lane_roll(east, -1)
        north, north_m, north_1 = (table[2, at(tile, n), :] for n in (0, -1, 1))
        for k in range(K):
            for dom in doms:
                here, grad = x[dom, k, at(tile), :], tz[dom, k, at(tile), :]
                if tile in tiles:
                    right, left = lane_roll(here, -1), lane_roll(here, 1)
                    far = lane_roll(here, -2)
                    grad_right = lane_roll(grad, -1)
                    jump = jnp.where(east > k, right - here, 0.0)
                    before = jnp.where(east_m > k, here - left, 0.0)
                    after = jnp.where(east_1 > k, far - right, 0.0)
                    fx[dom, k, plain(tile), :] = face_flux(
                        *(statics[i, k, plain(tile), :] for i in range(4)),
                        here, right, before, jump, after, grad + grad_right,
                    )
                    tx[dom, k, plain(tile), :] = before + jump
                up, down, far = (x[dom, k, at(tile, n), :] for n in (1, -1, 2))
                grads = grad + tz[dom, k, at(tile, 1), :]
                jump = jnp.where(north > k, up - here, 0.0)
                before = jnp.where(north_m > k, here - down, 0.0)
                after = jnp.where(north_1 > k, far - up, 0.0)
                fy[dom, k, at(tile), :] = face_flux(
                    *(statics[i, k, plain(tile), :] for i in range(4, 8)),
                    here, up, before, jump, after, grads,
                )
                ty[dom, k, plain(tile), :] = before + jump
                if tile == 2 and 3 in tiles:
                    fseam[dom, k] = face_flux(
                        *(seam[i, k] for i in range(4)), here, up, before, jump, after, grads
                    )


def sum_pass(x, later, doms, table, statics, dz, fx, fy, tx, ty, fseam, tiles):
    first_row = lax.broadcasted_iota(jnp.int32, (8, LANES), 0) == 0
    for tile in tiles:
        rows = plain(tile)
        level = table[0, at(tile), :]
        for dom in doms:
            flux_above = None
            here, d_above = x[dom, 0, at(tile), :], None
            tx_here, ty_here = tx[dom, 0, rows, :], ty[dom, 0, rows, :]
            for k in range(K):
                f = fx[dom, k, rows, :]
                total = lane_roll(f, 1) - f
                south = fy[dom, k, at(tile, -1), :]
                if tile == 3:
                    south = jnp.where(first_row, row_roll(fseam[dom, k], 1), south)
                total = total + (south - fy[dom, k, at(tile), :])
                if flux_above is not None:
                    total = total + flux_above
                if k < K - 1:
                    below = x[dom, k + 1, at(tile), :]
                    tx_below, ty_below = tx[dom, k + 1, rows, :], ty[dom, k + 1, rows, :]
                    d = dz[dom, k, rows, :]
                    d_below = dz[dom, k + 1, rows, :] if k < K - 2 else jnp.zeros_like(d)
                    before = jnp.zeros_like(d) if d_above is None else d_above
                    c, h, g, a, b = (statics[i, k, rows, :] for i in range(8, 13))
                    down = c > 0
                    slope = minmod(jnp.where(down, before, d_below), d)
                    flux = c * (jnp.where(down, here, below) + h * slope) - (
                        g * d + a * (tx_here + tx_below) + b * (ty_here + ty_below)
                    )
                    total = total - flux
                    flux_above, d_above = flux, d
                later[dom, k, at(tile), :] = here + jnp.where(level > k, total, 0.0)
                if k < K - 1:
                    here, tx_here, ty_here = below, tx_below, ty_below


def unpack_south(band, raw, x, lev):
    for k in range(K):
        for f in range(STATICS):
            raw[f, k, 4:8, :] = band[k, 4 * f : 4 * f + 4, :]
        for n, f in enumerate(NORTHWARD):
            raw[f, k, 3:4, :] = band[k, 52 + n : 53 + n, :]
        for t in range(2):
            x[t, k, 10:16, :] = band[k, 40 + 6 * t : 46 + 6 * t, :]
        if k < 6:
            lev[2 + k : 3 + k, :] = band[k, 55:56, :]


def unpack_north(band, raw, x, lev, seam):
    for k in range(K):
        for f in range(STATICS):
            raw[f, k, 24:28, :] = band[k, 4 * f : 4 * f + 4, :]
        for t in range(2):
            x[t, k, 32:38, :] = band[k, 40 + 6 * t : 46 + 6 * t, :]
        if k < 6:
            lev[24 + k : 25 + k, :] = band[k, 55:56, :]
        for n, f in enumerate(NORTHWARD):
            seam[n, k] = raw[f, k, 16:24, :]


def unpack_fold(band, flat, raw, x, lev, seam):
    mirror = LANES - 1 - lanes_of((8, LANES))
    for k in range(K):
        for g in range(7):
            rows = slice(8 * g, 8 * g + 8)
            flat[k, rows, :] = jnp.take_along_axis(band[k, rows, :], mirror, axis=1)
        for f in range(STATICS):
            sign = -1.0 if f in FLIPPED else 1.0
            if f in NORTHWARD:
                n = f - NORTHWARD[0]
                seam[n, k, 7:8, :] = sign * flat[k, 4 * f + 3 : 4 * f + 4, :]
                order = [4 * f + 2, 4 * f + 1, 4 * f, 52 + n]
            else:
                order = [4 * f + 3, 4 * f + 2, 4 * f + 1, 4 * f]
            for r, source in enumerate(order):
                raw[f, k, 24 + r : 25 + r, :] = sign * flat[k, source : source + 1, :]
        for t in range(2):
            for r in range(6):
                source = 45 + 6 * t - r
                x[t, k, 32 + r : 33 + r, :] = flat[k, source : source + 1, :]
        if k < 6:
            lev[29 - k : 30 - k, :] = flat[k, 55:56, :]


def step_kernel(tracers, levels, *refs):
    statics = refs[:STATICS]
    near, far, merged, near_corner, far_corner, out = refs[STATICS : STATICS + 6]
    (raw, flat, x, xb, lev, seam, derived, seam_derived,
     halo, sraw, slev, sseam, sderived, sseam_derived,
     table, stable, dz, tz, fx, fy, tx, ty, fseam) = refs[STATICS + 6 :]
    even, top = is_even("lat"), is_top()
    lane8 = lanes_of((8, LANES))

    for f in range(STATICS):
        for k in range(K):
            raw[f, k, 8:24, :] = statics[f][k]
    for t in range(2):
        for k in range(K):
            x[t, k, 16:32, :] = tracers[t, k]
    lev[8:24, :] = levels[...].astype(jnp.float32)
    for tile in range(2):
        for v in range(SLOTS):
            halo[1 + tile, v] = merged[tile, v]

    @pl.when(even)
    def _():
        unpack_south(far, raw, x, lev)
        unpack_north(near, raw, x, lev, seam)
        for v in range(SLOTS):
            halo[0, v] = far_corner[v]
            halo[3, v] = near_corner[v]

    @pl.when(jnp.logical_not(even))
    def _():
        unpack_south(near, raw, x, lev)
        for v in range(SLOTS):
            halo[0, v] = near_corner[v]

        @pl.when(top)
        def _():
            unpack_fold(far, flat, raw, x, lev, seam)
            flip = (lane8 // 16) * 16 + 15 - lane8 % 16
            for v in range(SLOTS):
                turned = jnp.take_along_axis(far_corner[v], flip, axis=1)
                for r in range(8):
                    halo[3, v, r : r + 1, :] = turned[7 - r : 8 - r, :]

        @pl.when(jnp.logical_not(top))
        def _():
            unpack_north(far, raw, x, lev, seam)
            for v in range(SLOTS):
                halo[3, v] = far_corner[v]

    half = lane8 % 64
    in_halo = (half >= 24) & (half < 40)
    low, first = half < 24, lane8 < 64

    def strip(own, packed, slot):
        both = jnp.where(low, lane_roll(own, 24), lane_roll(own, 40))
        return jnp.where(in_halo, lane_roll(packed, 24 - 16 * (slot % 8)), both)

    def twice(strip64):
        return jnp.where(first, strip64, lane_roll(strip64, 64))

    for tile in range(4):
        rows = plain(tile)
        for f in range(STATICS):
            for k in range(K):
                slot = f * K + k
                sraw[f, k, rows, :] = strip(raw[f, k, rows, :], halo[tile, slot // 8], slot)
        for k in range(K):
            x[2, k, at(tile), :] = strip(x[0, k, at(tile), :], halo[tile, (120 + k) // 8], 120 + k)
            tz[0, k, at(tile), :] = strip(x[1, k, at(tile), :], halo[tile, (132 + k) // 8], 132 + k)
        slev[rows, :] = twice(strip(lev[rows, :], halo[tile, 18], 144))
    for tile in range(4):
        rows = plain(tile)
        for f in range(STATICS):
            for k in range(K):
                sraw[f, k, rows, :] = twice(sraw[f, k, rows, :])
        for k in range(K):
            x[2, k, at(tile), :] = jnp.where(
                first, x[2, k, at(tile), :], lane_roll(tz[0, k, at(tile), :], 64)
            )
    for n, f in enumerate(NORTHWARD):
        for k in range(K):
            sseam[n, k] = sraw[f, k, 16:24, :]

    @pl.when(top)
    def _():
        for f in range(STATICS):
            for k in range(K):
                slot = f * K + k
                v = sraw[f, k, 24:32, :]
                if f in FLIPPED:
                    v = jnp.where(in_halo, -v, v)
                if f in NORTHWARD:
                    n = f - NORTHWARD[0]
                    own = strip(seam[n, k], halo[3, slot // 8], slot)
                    sign = -1.0 if f in FLIPPED else 1.0
                    packed = lane_roll(halo[3, slot // 8], 24 - 16 * (slot % 8))
                    last = jnp.where(in_halo[:1], sign * packed[:1], own[7:8])
                    sseam[n, k, 7:8, :] = twice(jnp.concatenate([last] * 8, axis=0))[:1]
                    moved = row_roll(v, -1)
                    v = jnp.where(in_halo, moved, v)
                if f in EASTWARD:
                    v = lane_roll(v, -1)
                    raw[f, k, 24:32, :] = lane_roll(raw[f, k, 24:32, :], -1)
                sraw[f, k, 24:32, :] = v

    level_tables(lev[...], table)
    level_tables(slev[...], stable)
    derive(raw, derived, seam, seam_derived, table)
    derive(sraw, sderived, sseam, sseam_derived, stable)

    now, later = x, xb
    for step in range(STEPS):
        tiles = (1, 2) if step == STEPS - 1 else (0, 1, 2, 3)
        for doms, tab, der, sea in (
            ((0, 1), table, derived, seam_derived),
            ((2,), stable, sderived, sseam_derived),
        ):
            grads_pass(now, doms, tab, dz, tz)
            sides_pass(now, doms, tab, der, sea, tz, fx, fy, tx, ty, fseam, tiles)
            sum_pass(now, later, doms, tab, der, dz, fx, fy, tx, ty, fseam, tiles)
        now, later = later, now

    lane = lanes_of((8, LANES))
    for t in range(2):
        for k in range(K):
            for tile in (1, 2):
                s = now[2, k, at(tile), :]
                west, east = lane_roll(s, -40 - 64 * t), lane_roll(s, 104 - 64 * t)
                mid = now[t, k, at(tile), :]
                out[t, k, plain(tile - 1), :] = jnp.where(
                    lane < 6, west, jnp.where(lane >= 122, east, mid)
                )


def swaps(count, first, wrap):
    pairs = []
    for low in range(first, count if wrap else count - 1, 2):
        high = (low + 1) % count
        pairs += [(low, high), (high, low)]
    return pairs


def swap_lon(array):
    count = lax.axis_size("lon")
    return (
        lax.ppermute(array, "lon", swaps(count, 0, False)),
        lax.ppermute(array, "lon", swaps(count, 1, True)),
    )


def swap_lat(near, far):
    bands, count = lax.axis_size("lat"), lax.axis_size("lon")
    pairs = [
        (low * count + i, high * count + i)
        for low, high in swaps(bands, 1, False)
        for i in range(count)
    ]
    last = (bands - 1) * count
    pairs += [(last + i, last + count - 1 - i) for i in range(count)]
    return (
        lax.ppermute(near, "lat", swaps(bands, 0, False)),
        lax.ppermute(far, ("lat", "lon"), pairs),
    )


def shape(*dims):
    return jax.ShapeDtypeStruct(dims, jnp.float32)


def params(limit=VMEM_LIMIT):
    return pltpu.CompilerParams(vmem_limit_bytes=limit)


def body(tracers, wet_levels, ce, cn, cd, de, se, dn, sn, dd, dse, dsn):
    statics = (ce, de, se, cn, dn, sn, cd, dd, dse, dsn)
    sides = pl.pallas_call(
        side_kernel,
        out_shape=shape(2, SLOTS, 8, LANES),
        compiler_params=params(FULL),
        name="sides",
    )(tracers, wet_levels, *statics)
    near_side, far_side = swap_lon(sides)
    in_vmem = pl.BlockSpec(memory_space=pltpu.VMEM)
    near, far = pl.pallas_call(
        band_kernel,
        out_shape=(shape(K, 56, LANES), shape(K, 56, LANES)),
        in_specs=[in_vmem] * (2 + STATICS) + [pl.BlockSpec(memory_space=pl.ANY)],
        compiler_params=params(FULL),
        name="bands",
    )(tracers, wet_levels, *statics, far_side)
    near, far = swap_lat(near, far)
    merged, near_corner, far_corner = pl.pallas_call(
        corner_kernel,
        out_shape=(shape(2, SLOTS, 8, LANES), shape(SLOTS, 8, LANES), shape(SLOTS, 8, LANES)),
        compiler_params=params(),
        name="corners",
    )(near_side, far_side)
    near_corner, far_corner = swap_lat(near_corner, far_corner)
    return pl.pallas_call(
        step_kernel,
        out_shape=shape(2, K, ROWS, LANES),
        scratch_shapes=[
            pltpu.VMEM(dims, jnp.float32)
            for dims in (
                (STATICS, K, EXT, LANES),
                (K, 56, LANES),
                (3, K, PAD, LANES),
                (3, K, PAD, LANES),
                (EXT, LANES),
                (3, K, 8, LANES),
                (13, K, EXT, LANES),
                (4, K, 8, LANES),
                (4, SLOTS, 8, LANES),
                (STATICS, K, EXT, LANES),
                (EXT, LANES),
                (3, K, 8, LANES),
                (13, K, EXT, LANES),
                (4, K, 8, LANES),
                (3, PAD, LANES),
                (3, PAD, LANES),
                (3, K, EXT, LANES),
                (3, K, PAD, LANES),
                (3, K, EXT, LANES),
                (3, K, PAD, LANES),
                (3, K, EXT, LANES),
                (3, K, EXT, LANES),
                (3, K, 8, LANES),
            )
        ],
        compiler_params=params(),
        name="steps",
    )(tracers, wet_levels, *statics, near, far, merged, near_corner, far_corner)


def solution(mesh):
    field = P(None, "lat", "lon")
    whole = P(None, None, "lat", "lon")
    in_specs = (whole, P("lat", "lon")) + (field,) * STATICS
    return jax.shard_map(body, mesh=mesh, in_specs=in_specs, out_specs=whole, check_vma=False)
```

profile of v0, /device:TPU:14, one launch (start us, length us, event | category | flops | bytes accessed | tf_op | source)
XLA Modules:
  0.0 50.7 jit_solution(16654257099564998153)
XLA Ops:
  0.0 2.4 %sides.1 = f32[2,19,8,128]{3,2,1,0:T(8,128)} custom-call(f32[2,12,16,128]{3,2,1,0:T(8,128)} %tracers.5, s32[16,128]{1,0:T(8,128)} %levels.5, f32[12,16,128]{2,1,0:T(8,128)} %refs_0_.5, f32[12,16,128]{2,1,0:T(8,128)} %refs_1_.5, f32[12,16,128]{2,1,0:T(8,128)} %refs_2_.5, f32[12,16,128]{2,1,0:T(8,128)} %refs_3_.5, f32[12,16,128]{2,1,0:T(8,128)} %refs_4_.5, ...), custom_call_target="tpu_custom_call" | custom-call | tf_op jit(solution)/shard_map/sides/pallas_call | solution.py:486
  2.4 7.0 %collective-permute-start = (f32[2,19,8,128]{3,2,1,0:T(8,128)}, f32[2,19,8,128]{3,2,1,0:T(8,128)}, u32[]{:S(2)}, u32[]{:S(2)}) collective-permute-start(f32[2,19,8,128]{3,2,1,0:T(8,128)} %sides.1), channel_id=1, source_target_pairs={{1,2},{2,1},{3,4},{4,3},{5,6},{6,5},{7,8},{8,7},{9,10},{10,9},{11,... | collective-permute-start | bytes 466952 | tf_op jit(solution)/shard_map/ppermute | solution.py:457
  9.4 3.2 %collective-permute-done.refs_10_.far_side = f32[2,19,8,128]{3,2,1,0:T(8,128)} collective-permute-done((f32[2,19,8,128]{3,2,1,0:T(8,128)}, f32[2,19,8,128]{3,2,1,0:T(8,128)}, u32[]{:S(2)}, u32[]{:S(2)}) %collective-permute-start) | collective-permute-done | bytes 155680 | tf_op jit(solution)/shard_map/ppermute | solution.py:457
  12.6 0.0 copy-start.2
  12.6 0.0 copy-start.3
  12.6 0.0 copy-start.4
  12.6 0.0 copy-start.5
  12.6 0.0 copy-start.6
  12.7 0.0 copy-start.7
  12.7 0.0 copy-start.8
  12.7 0.0 copy-start.9
  12.7 0.0 copy-start.10
  12.7 2.4 %bands.1 = (f32[12,56,128]{2,1,0:T(8,128)}, f32[12,56,128]{2,1,0:T(8,128)}) custom-call(f32[2,12,16,128]{3,2,1,0:T(8,128)} %tracers.5, s32[16,128]{1,0:T(8,128)} %levels.5, f32[12,16,128]{2,1,0:T(8,128)} %refs_0_.5, f32[12,16,128]{2,1,0:T(8,128)} %refs_1_.5, f32[12,16,128]{2,1,0:T(8,128)} %refs_2_.5, f32[12,16,128]{2,1,0:T(8,128)} %refs_3_.5, ...), custom_call_target="tpu_custom_call" | custom-call | tf_op jit(solution)/shard_map/bands/pallas_call | solution.py:494
  15.2 0.0 copy-start
  15.2 1.4 %collective-permute-start.1 = (f32[12,56,128]{2,1,0:T(8,128)}, f32[12,56,128]{2,1,0:T(8,128)S(1)}, u32[]{:S(2)}, u32[]{:S(2)}) collective-permute-start(f32[12,56,128]{2,1,0:T(8,128)} %get-tuple-element.10), channel_id=1, source_target_pairs={{0,32},{32,0},{64,96},{96,64},{128,160},{160,128},{192,224},{224,1... | collective-permute-start | bytes 1032200 | tf_op jit(solution)/shard_map/ppermute | solution.py:471
  16.5 0.0 copy-start.1
  16.5 6.5 %collective-permute-start.2 = (f32[12,56,128]{2,1,0:T(8,128)}, f32[12,56,128]{2,1,0:T(8,128)S(1)}, u32[]{:S(2)}, u32[]{:S(2)}) collective-permute-start(f32[12,56,128]{2,1,0:T(8,128)} %get-tuple-element.11), channel_id=1, source_target_pairs={{32,64},{33,65},{34,66},{35,67},{36,68},{37,69},{38,70},{39,71},{4... | collective-permute-start | bytes 1032200 | tf_op jit(solution)/shard_map/ppermute | solution.py:472
  23.0 0.1 collective-permute-start.3
  23.1 1.6 %collective-permute-done.3.near_side = f32[2,19,8,128]{3,2,1,0:T(8,128)S(1)} collective-permute-done((f32[2,19,8,128]{3,2,1,0:T(8,128)}, f32[2,19,8,128]{3,2,1,0:T(8,128)S(1)}, u32[]{:S(2)}, u32[]{:S(2)}) %collective-permute-start.3) | collective-permute-done | bytes 155680 | tf_op jit(solution)/shard_map/ppermute | solution.py:456
  24.7 0.0 copy-start.11
  24.7 1.1 %corners.1 = (f32[2,19,8,128]{3,2,1,0:T(8,128)S(1)}, f32[19,8,128]{2,1,0:T(8,128)S(1)}, f32[19,8,128]{2,1,0:T(8,128)S(1)}) custom-call(f32[2,19,8,128]{3,2,1,0:T(8,128)S(1)} %collective-permute-done.3.near_side, f32[2,19,8,128]{3,2,1,0:T(8,128)} %collective-permute-done.refs_10_.far_side), custom_call_target="tpu_custom_call" | custom-call | tf_op jit(solution)/shard_map/corners/pallas_call | solution.py:502
  25.8 0.1 collective-permute-start.4
  25.9 3.6 %collective-permute-start.5 = (f32[19,8,128]{2,1,0:T(8,128)S(1)}, f32[19,8,128]{2,1,0:T(8,128)S(1)}, u32[]{:S(2)}, u32[]{:S(2)}) collective-permute-start(f32[19,8,128]{2,1,0:T(8,128)S(1)} %get-tuple-element.14), channel_id=1, source_target_pairs={{32,64},{33,65},{34,66},{35,67},{36,68},{37,69},{38,70},{39,71},{4... | collective-permute-start | bytes 233480 | tf_op jit(solution)/shard_map/ppermute | solution.py:472
  29.5 9.1 %collective-permute-done.4.refs_13_ = f32[19,8,128]{2,1,0:T(8,128)S(1)} collective-permute-done((f32[19,8,128]{2,1,0:T(8,128)S(1)}, f32[19,8,128]{2,1,0:T(8,128)S(1)}, u32[]{:S(2)}, u32[]{:S(2)}) %collective-permute-start.4) | collective-permute-done | bytes 77856 | tf_op jit(solution)/shard_map/ppermute | solution.py:471
  38.6 1.1 %collective-permute-done.5.refs_14_ = f32[19,8,128]{2,1,0:T(8,128)S(1)} collective-permute-done((f32[19,8,128]{2,1,0:T(8,128)S(1)}, f32[19,8,128]{2,1,0:T(8,128)S(1)}, u32[]{:S(2)}, u32[]{:S(2)}) %collective-permute-start.5) | collective-permute-done | bytes 77856 | tf_op jit(solution)/shard_map/ppermute | solution.py:472
  39.7 0.0 collective-permute-done.1.refs_10_
  39.7 0.0 collective-permute-done.2.refs_11_
  39.7 0.0 copy-done.2
  39.7 0.0 copy-done.3
  39.7 0.0 copy-done.4
  39.7 0.0 copy-done.5
  39.8 0.0 copy-done.6
  39.8 0.0 copy-done.7
  39.8 0.0 copy-done.8
  39.8 0.0 copy-done.9
  39.8 0.0 copy-done.10
  39.8 0.0 copy-done
  39.8 0.0 copy-done.1
  39.8 0.0 copy-done.11
  39.8 10.9 %steps.1 = f32[2,12,16,128]{3,2,1,0:T(8,128)} custom-call(f32[2,12,16,128]{3,2,1,0:T(8,128)S(1)} %copy-done, s32[16,128]{1,0:T(8,128)S(1)} %copy-done.11, f32[12,16,128]{2,1,0:T(8,128)S(1)} %copy-done.1, f32[12,16,128]{2,1,0:T(8,128)S(1)} %copy-done.2, f32[12,16,128]{2,1,0:T(8,128)S(1)} %copy-done.3, f32[12,16,128]{2,1,0:T(8,128)S(1)} %copy-done.4, ...), custom_call_target="tpu_custom_call" | custom-call | tf_op jit(solution)/shard_map/steps/pallas_call | solution.py:509
Async XLA Ops:
  2.4 10.3 %collective-permute-start = (f32[2,19,8,128]{3,2,1,0:T(8,128)}, f32[2,19,8,128]{3,2,1,0:T(8,128)}, u32[]{:S(2)}, u32[]{:S(2)}) collective-permute-start(f32[2,19,8,128]{3,2,1,0:T(8,128)} %sides.1), channel_id=1, source_target_pairs={{1,2},{2,1},{3,4},{4,3},{5,6},{6,5},{7,8},{8,7},{9,10},{10,9},{11,... | collective-permute-start | bytes 466952 | tf_op jit(solution)/shard_map/ppermute | solution.py:457
  12.6 27.1 %copy-start.2 = (f32[12,16,128]{2,1,0:T(8,128)S(1)}, f32[12,16,128]{2,1,0:T(8,128)}, u32[]{:S(2)}) copy-start(f32[12,16,128]{2,1,0:T(8,128)} %refs_1_.5) | copy-start | bytes 294916
  12.6 27.1 %copy-start.3 = (f32[12,16,128]{2,1,0:T(8,128)S(1)}, f32[12,16,128]{2,1,0:T(8,128)}, u32[]{:S(2)}) copy-start(f32[12,16,128]{2,1,0:T(8,128)} %refs_2_.5) | copy-start | bytes 294916
  12.6 27.1 %copy-start.4 = (f32[12,16,128]{2,1,0:T(8,128)S(1)}, f32[12,16,128]{2,1,0:T(8,128)}, u32[]{:S(2)}) copy-start(f32[12,16,128]{2,1,0:T(8,128)} %refs_3_.5) | copy-start | bytes 294916
  12.6 27.1 %copy-start.5 = (f32[12,16,128]{2,1,0:T(8,128)S(1)}, f32[12,16,128]{2,1,0:T(8,128)}, u32[]{:S(2)}) copy-start(f32[12,16,128]{2,1,0:T(8,128)} %refs_4_.5) | copy-start | bytes 294916
  12.6 27.1 %copy-start.6 = (f32[12,16,128]{2,1,0:T(8,128)S(1)}, f32[12,16,128]{2,1,0:T(8,128)}, u32[]{:S(2)}) copy-start(f32[12,16,128]{2,1,0:T(8,128)} %refs_5_.5) | copy-start | bytes 294916
  12.7 27.1 %copy-start.7 = (f32[12,16,128]{2,1,0:T(8,128)S(1)}, f32[12,16,128]{2,1,0:T(8,128)}, u32[]{:S(2)}) copy-start(f32[12,16,128]{2,1,0:T(8,128)} %refs_6_.5) | copy-start | bytes 294916
  12.7 27.1 %copy-start.8 = (f32[12,16,128]{2,1,0:T(8,128)S(1)}, f32[12,16,128]{2,1,0:T(8,128)}, u32[]{:S(2)}) copy-start(f32[12,16,128]{2,1,0:T(8,128)} %refs_7_.5) | copy-start | bytes 294916
  12.7 27.1 %copy-start.9 = (f32[12,16,128]{2,1,0:T(8,128)S(1)}, f32[12,16,128]{2,1,0:T(8,128)}, u32[]{:S(2)}) copy-start(f32[12,16,128]{2,1,0:T(8,128)} %refs_8_.5) | copy-start | bytes 294916
  12.7 27.1 %copy-start.10 = (f32[12,16,128]{2,1,0:T(8,128)S(1)}, f32[12,16,128]{2,1,0:T(8,128)}, u32[]{:S(2)}) copy-start(f32[12,16,128]{2,1,0:T(8,128)} %refs_9_.5) | copy-start | bytes 294916
  15.2 24.6 %copy-start = (f32[2,12,16,128]{3,2,1,0:T(8,128)S(1)}, f32[2,12,16,128]{3,2,1,0:T(8,128)}, u32[]{:S(2)}) copy-start(f32[2,12,16,128]{3,2,1,0:T(8,128)} %tracers.5) | copy-start | bytes 589828
  15.2 24.6 %collective-permute-start.1 = (f32[12,56,128]{2,1,0:T(8,128)}, f32[12,56,128]{2,1,0:T(8,128)S(1)}, u32[]{:S(2)}, u32[]{:S(2)}) collective-permute-start(f32[12,56,128]{2,1,0:T(8,128)} %get-tuple-element.10), channel_id=1, source_target_pairs={{0,32},{32,0},{64,96},{96,64},{128,160},{160,128},{192,224},{224,1... | collective-permute-start | bytes 1032200 | tf_op jit(solution)/shard_map/ppermute | solution.py:471
  16.5 23.3 %copy-start.1 = (f32[12,16,128]{2,1,0:T(8,128)S(1)}, f32[12,16,128]{2,1,0:T(8,128)}, u32[]{:S(2)}) copy-start(f32[12,16,128]{2,1,0:T(8,128)} %refs_0_.5) | copy-start | bytes 294916
  16.5 23.2 %collective-permute-start.2 = (f32[12,56,128]{2,1,0:T(8,128)}, f32[12,56,128]{2,1,0:T(8,128)S(1)}, u32[]{:S(2)}, u32[]{:S(2)}) collective-permute-start(f32[12,56,128]{2,1,0:T(8,128)} %get-tuple-element.11), channel_id=1, source_target_pairs={{32,64},{33,65},{34,66},{35,67},{36,68},{37,69},{38,70},{39,71},{4... | collective-permute-start | bytes 1032200 | tf_op jit(solution)/shard_map/ppermute | solution.py:472
  23.0 1.7 %collective-permute-start.3 = (f32[2,19,8,128]{3,2,1,0:T(8,128)}, f32[2,19,8,128]{3,2,1,0:T(8,128)S(1)}, u32[]{:S(2)}, u32[]{:S(2)}) collective-permute-start(f32[2,19,8,128]{3,2,1,0:T(8,128)} %sides.1), channel_id=1, source_target_pairs={{0,1},{1,0},{2,3},{3,2},{4,5},{5,4},{6,7},{7,6},{8,9},{9,8},{10,11... | collective-permute-start | bytes 466952 | tf_op jit(solution)/shard_map/ppermute | solution.py:456
  24.7 15.1 %copy-start.11 = (s32[16,128]{1,0:T(8,128)S(1)}, s32[16,128]{1,0:T(8,128)}, u32[]{:S(2)}) copy-start(s32[16,128]{1,0:T(8,128)} %levels.5) | copy-start | bytes 24580
  25.8 12.8 %collective-permute-start.4 = (f32[19,8,128]{2,1,0:T(8,128)S(1)}, f32[19,8,128]{2,1,0:T(8,128)S(1)}, u32[]{:S(2)}, u32[]{:S(2)}) collective-permute-start(f32[19,8,128]{2,1,0:T(8,128)S(1)} %get-tuple-element.13), channel_id=1, source_target_pairs={{0,32},{32,0},{64,96},{96,64},{128,160},{160,128},{192,224},{224,1... | collective-permute-start | bytes 233480 | tf_op jit(solution)/shard_map/ppermute | solution.py:471
  25.9 13.8 %collective-permute-start.5 = (f32[19,8,128]{2,1,0:T(8,128)S(1)}, f32[19,8,128]{2,1,0:T(8,128)S(1)}, u32[]{:S(2)}, u32[]{:S(2)}) collective-permute-start(f32[19,8,128]{2,1,0:T(8,128)S(1)} %get-tuple-element.14), channel_id=1, source_target_pairs={{32,64},{33,65},{34,66},{35,67},{36,68},{37,69},{38,70},{39,71},{4... | collective-permute-start | bytes 233480 | tf_op jit(solution)/shard_map/ppermute | solution.py:472
where the time goes:
time: 50.9 us; the launch traced here: 50.7 us
  starting transfers between devices  18.7 us (37%)
  Pallas kernels  16.8 us (33%)
  waiting for transfers between devices  15 us (29%)
    pallas_call x1, Pallas kernels, body(): pl.pallas_call(step_kernel, out_shape=shape(2, K, ROWS, LANES), scratch_s...  10.9 us
    ppermute x2, starting transfers between devices, swap_lat(): lax.ppermute(far, ('lat', 'lon'), pairs)  10.1 us
    ppermute x2, waiting for transfers between devices, swap_lat(): lax.ppermute(near, 'lat', swaps(bands, 0, False))  9.08 us
    ppermute x1, starting transfers between devices, swap_lon(): lax.ppermute(array, 'lon', swaps(count, 1, True))  7.03 us
    ppermute x1, waiting for transfers between devices, swap_lon(): lax.ppermute(array, 'lon', swaps(count, 1, True))  3.23 us
    pallas_call x1, Pallas kernels, body(): pl.pallas_call(band_kernel, out_shape=(shape(K, 56, LANES), shape(K, 56,...  2.45 us
    pallas_call x1, Pallas kernels, body(): pl.pallas_call(side_kernel, out_shape=shape(2, SLOTS, 8, LANES), compiler...  2.38 us
    ppermute x1, waiting for transfers between devices, swap_lon(): lax.ppermute(array, 'lon', swaps(count, 0, False))  1.58 us
  transfers between devices with their start and end apart: 6, of which 4 were waited for; matrix products, arithmetic and copies ran while one was open for 0% of the time, Pallas kernels for 2%

commit v1 on v0

v1 whole, which is shorter than its diff:
```python
import jax
import jax.numpy as jnp
from jax import lax
from jax.experimental import pallas as pl
from jax.experimental.pallas import tpu as pltpu
from jax.sharding import PartitionSpec as P

STEPS = 3
K = 12
ROWS = 16
LANES = 128
EXT = 32
PAD = 48
NORTHWARD = (3, 4, 5)
EASTWARD = (0, 1, 2)
FLIPPED = (0, 2, 3, 5, 8, 9)
STATICS = 10
SLOTS = 19
HALVES = 10
BAND = 56
VMEM_LIMIT = 48 * 1024 * 1024
FULL = 63 * 1024 * 1024


def lane_roll(x, shift):
    return pltpu.roll(x, shift % x.shape[-1], x.ndim - 1)


def row_roll(x, shift):
    return pltpu.roll(x, shift % x.shape[0], 0)


def lanes_of(shape):
    return lax.broadcasted_iota(jnp.int32, shape, len(shape) - 1)


def is_even(axis):
    return lax.rem(lax.axis_index(axis), 2) == 0


def is_top():
    return lax.axis_index("lat") == lax.axis_size("lat") - 1


def at_band(k, row, count):
    return slice(BAND * k + row, BAND * k + row + count)


def pack_band(dst, tracers, levels, statics, northward):
    low4 = ROWS - 4 if northward else 0
    low6 = ROWS - 6 if northward else 0
    extra = ROWS - 5 if northward else 0
    for k in range(K):
        for f in range(STATICS):
            dst[at_band(k, 4 * f, 4), :] = statics[f][k, low4 : low4 + 4, :]
        for t in range(2):
            dst[at_band(k, 40 + 6 * t, 6), :] = tracers[t, k, low6 : low6 + 6, :]
        for n, f in enumerate(NORTHWARD):
            dst[at_band(k, 52 + n, 1), :] = statics[f][k, extra : extra + 1, :]
        row = low6 + k if k < 6 else 0
        dst[at_band(k, 55, 1), :] = levels[row : row + 1, :].astype(jnp.float32)


def pack_kernel(tracers, levels, *refs):
    statics = refs[:STATICS]
    near, far, near_own, far_own, packed_all = refs[STATICS:]
    even = is_even("lat")

    @pl.when(even)
    def _():
        pack_band(near, tracers, levels, statics, True)
        pack_band(far, tracers, levels, statics, False)

    @pl.when(jnp.logical_not(even))
    def _():
        pack_band(far, tracers, levels, statics, True)
        pack_band(near, tracers, levels, statics, False)

    pack_sides(
        (1, 2), statics, tracers, None, None,
        lambda tile: levels[plain(tile - 1), :].astype(jnp.float32), near_own, far_own, packed_all,
    )


def pack_sides(tiles, statics, tracers, raw, x, level_of, near_side, far_side, packed_all):
    even_lon = is_even("lon")
    place = lanes_of((8, LANES)) // 16
    low = lanes_of((8, LANES)) % 16 < 8
    for at_tile, tile in enumerate(tiles):
        for v in range(SLOTS):
            packed = jnp.zeros((8, LANES), jnp.float32)
            for q in range(8):
                slot = 8 * v + q
                f, k = slot // K, slot % K
                if slot > 12 * K:
                    continue
                if slot == 12 * K:
                    value = level_of(tile)
                elif f < STATICS:
                    value = tile_of(statics, raw, (f, k), tile)
                else:
                    value = tile_of(tracers, x, (f - STATICS, k), tile)
                packed = jnp.where(place == q, lane_roll(value, 8 + 16 * q), packed)
            packed_all[at_tile, v] = packed
        packed_all[at_tile, SLOTS] = jnp.zeros((8, LANES), jnp.float32)
        for u in range(HALVES):
            one, two = packed_all[at_tile, 2 * u], packed_all[at_tile, 2 * u + 1]
            eastern = jnp.where(low, one, lane_roll(two, 8))
            western = jnp.where(low, lane_roll(one, -8), two)
            near_side[at_tile, u] = jnp.where(even_lon, eastern, western)
            far_side[at_tile, u] = jnp.where(even_lon, western, eastern)


def expand(halo, tile, u, near, far, western_near):
    low = lanes_of((8, LANES)) % 16 < 8
    western = jnp.where(western_near, near, far)
    eastern = jnp.where(western_near, far, near)
    halo[tile, 2 * u] = jnp.where(low, western, lane_roll(eastern, 8))
    halo[tile, 2 * u + 1] = jnp.where(low, lane_roll(western, -8), eastern)


def minmod(p, q):
    return jnp.maximum(jnp.minimum(p, q), 0.0) + jnp.minimum(jnp.maximum(p, q), 0.0)


def signed_half(c):
    return jnp.where(c > 0, 0.5, -0.5) - 0.5 * c


def face_flux(c, h, spread, tilt, here, there, before, jump, after, grads):
    up = c > 0
    slope = minmod(jnp.where(up, before, after), jump)
    return c * (jnp.where(up, here, there) + h * slope) - spread * (jump + tilt * grads)


def at(tile, shift=0):
    return slice(8 + 8 * tile + shift, 16 + 8 * tile + shift)


def plain(tile):
    return slice(8 * tile, 8 * tile + 8)


def level_tables(level, table):
    table[0, 8 : 8 + EXT, :] = level
    table[1, 8 : 8 + EXT, :] = jnp.minimum(level, lane_roll(level, -1))
    table[2, 8 : 8 + EXT, :] = jnp.minimum(level, row_roll(level, -1))


def derive(raw, put, seam_put, table):
    for tile in range(4):
        rows = plain(tile)
        level, east_level, north_level = (table[i, at(tile), :] for i in range(3))
        for k in range(K):
            east, north, lower = east_level > k, north_level > k, level > k + 1
            c = raw[0, k, rows, :]
            put[0, k, rows, :] = jnp.where(east, c, 0.0)
            put[1, k, rows, :] = signed_half(c)
            put[2, k, rows, :] = raw[1, k, rows, :]
            put[3, k, rows, :] = jnp.where(east, 0.25 * raw[2, k, rows, :], 0.0)
            c = raw[3, k, rows, :]
            put[4, k, rows, :] = jnp.where(north, c, 0.0)
            put[5, k, rows, :] = signed_half(c)
            put[6, k, rows, :] = raw[4, k, rows, :]
            put[7, k, rows, :] = jnp.where(north, 0.25 * raw[5, k, rows, :], 0.0)
            if tile == 2:
                c = raw[3, k, 24:32, :]
                seam_put[0, k] = jnp.where(north, c, 0.0)
                seam_put[1, k] = signed_half(c)
                seam_put[2, k] = raw[4, k, 24:32, :]
                seam_put[3, k] = jnp.where(north, 0.25 * raw[5, k, 24:32, :], 0.0)
            if k < K - 1:
                c, spread = raw[6, k, rows, :], raw[7, k, rows, :]
                along, across = raw[8, k, rows, :], raw[9, k, rows, :]
                put[8, k, rows, :] = jnp.where(lower, c, 0.0)
                put[9, k, rows, :] = signed_half(c)
                put[10, k, rows, :] = spread * (along * along + across * across)
                masked = jnp.where(lower, 0.25 * spread, 0.0)
                put[11, k, rows, :] = masked * along
                put[12, k, rows, :] = masked * across


def grads_pass(x, doms, table, dz, tz):
    for tile in range(4):
        level = table[0, at(tile), :]
        for dom in doms:
            above = None
            here = x[dom, 0, at(tile), :]
            for k in range(K):
                if k < K - 1:
                    below = x[dom, k + 1, at(tile), :]
                    d = jnp.where(level > k + 1, below - here, 0.0)
                    dz[dom, k, plain(tile), :] = d
                    tz[dom, k, at(tile), :] = d if above is None else above + d
                    here, above = below, d
                else:
                    tz[dom, k, at(tile), :] = above


def sides_pass(x, doms, table, statics, seam, tz, fx, fy, tx, ty, fseam, tiles):
    for tile in range(4):
        if tile not in tiles and tile + 1 not in tiles:
            continue
        east = table[1, at(tile), :]
        east_m, east_1 = lane_roll(east, 1), lane_roll(east, -1)
        north, north_m, north_1 = (table[2, at(tile, n), :] for n in (0, -1, 1))
        for k in range(K):
            for dom in doms:
                here, grad = x[dom, k, at(tile), :], tz[dom, k, at(tile), :]
                if tile in tiles:
                    right, left = lane_roll(here, -1), lane_roll(here, 1)
                    far = lane_roll(here, -2)
                    grad_right = lane_roll(grad, -1)
                    jump = jnp.where(east > k, right - here, 0.0)
                    before = jnp.where(east_m > k, here - left, 0.0)
                    after = jnp.where(east_1 > k, far - right, 0.0)
                    fx[dom, k, plain(tile), :] = face_flux(
                        *(statics[i, k, plain(tile), :] for i in range(4)),
                        here, right, before, jump, after, grad + grad_right,
                    )
                    tx[dom, k, plain(tile), :] = before + jump
                up, down, far = (x[dom, k, at(tile, n), :] for n in (1, -1, 2))
                grads = grad + tz[dom, k, at(tile, 1), :]
                jump = jnp.where(north > k, up - here, 0.0)
                before = jnp.where(north_m > k, here - down, 0.0)
                after = jnp.where(north_1 > k, far - up, 0.0)
                fy[dom, k, at(tile), :] = face_flux(
                    *(statics[i, k, plain(tile), :] for i in range(4, 8)),
                    here, up, before, jump, after, grads,
                )
                ty[dom, k, plain(tile), :] = before + jump
                if tile == 2 and 3 in tiles:
                    fseam[dom, k] = face_flux(
                        *(seam[i, k] for i in range(4)), here, up, before, jump, after, grads
                    )


def sum_pass(x, later, doms, table, statics, dz, fx, fy, tx, ty, fseam, tiles):
    first_row = lax.broadcasted_iota(jnp.int32, (8, LANES), 0) == 0
    for tile in tiles:
        rows = plain(tile)
        level = table[0, at(tile), :]
        for dom in doms:
            flux_above = None
            here, d_above = x[dom, 0, at(tile), :], None
            tx_here, ty_here = tx[dom, 0, rows, :], ty[dom, 0, rows, :]
            for k in range(K):
                f = fx[dom, k, rows, :]
                total = lane_roll(f, 1) - f
                south = fy[dom, k, at(tile, -1), :]
                if tile == 3:
                    south = jnp.where(first_row, row_roll(fseam[dom, k], 1), south)
                total = total + (south - fy[dom, k, at(tile), :])
                if flux_above is not None:
                    total = total + flux_above
                if k < K - 1:
                    below = x[dom, k + 1, at(tile), :]
                    tx_below, ty_below = tx[dom, k + 1, rows, :], ty[dom, k + 1, rows, :]
                    d = dz[dom, k, rows, :]
                    d_below = dz[dom, k + 1, rows, :] if k < K - 2 else jnp.zeros_like(d)
                    before = jnp.zeros_like(d) if d_above is None else d_above
                    c, h, g, a, b = (statics[i, k, rows, :] for i in range(8, 13))
                    down = c > 0
                    slope = minmod(jnp.where(down, before, d_below), d)
                    flux = c * (jnp.where(down, here, below) + h * slope) - (
                        g * d + a * (tx_here + tx_below) + b * (ty_here + ty_below)
                    )
                    total = total - flux
                    flux_above, d_above = flux, d
                later[dom, k, at(tile), :] = here + jnp.where(level > k, total, 0.0)
                if k < K - 1:
                    here, tx_here, ty_here = below, tx_below, ty_below


def unpack_south(band, raw, x, lev):
    for k in range(K):
        for f in range(STATICS):
            raw[f, k, 4:8, :] = band[at_band(k, 4 * f, 4), :]
        for n, f in enumerate(NORTHWARD):
            raw[f, k, 3:4, :] = band[at_band(k, 52 + n, 1), :]
        for t in range(2):
            x[t, k, 2:8, :] = band[at_band(k, 40 + 6 * t, 6), :]
        if k < 6:
            lev[2 + k : 3 + k, :] = band[at_band(k, 55, 1), :]


def unpack_north(band, raw, x, lev):
    for k in range(K):
        for f in range(STATICS):
            raw[f, k, 8:12, :] = band[at_band(k, 4 * f, 4), :]
        for t in range(2):
            x[t, k, 8:14, :] = band[at_band(k, 40 + 6 * t, 6), :]
        if k < 6:
            lev[8 + k : 9 + k, :] = band[at_band(k, 55, 1), :]


def unpack_fold(band, flat, raw, x, lev):
    mirror = LANES - 1 - lanes_of((8, LANES))
    for k in range(K):
        for g in range(7):
            rows = slice(8 * g, 8 * g + 8)
            flat[k, rows, :] = jnp.take_along_axis(band[at_band(k, 8 * g, 8), :], mirror, axis=1)
        for f in range(STATICS):
            sign = -1.0 if f in FLIPPED else 1.0
            order = [4 * f + 3, 4 * f + 2, 4 * f + 1, 4 * f]
            if f in NORTHWARD:
                raw[f, k, 15:16, :] = sign * flat[k, order[0] : order[0] + 1, :]
                order = order[1:] + [52 + f - NORTHWARD[0]]
            for r, source in enumerate(order):
                raw[f, k, 8 + r : 9 + r, :] = sign * flat[k, source : source + 1, :]
        for t in range(2):
            for r in range(6):
                source = 45 + 6 * t - r
                x[t, k, 8 + r : 9 + r, :] = flat[k, source : source + 1, :]
        if k < 6:
            lev[13 - k : 14 - k, :] = flat[k, 55:56, :]


def middle_kernel(near, far, *refs):
    raw, x, lev, near_side, far_side, flat, packed_all = refs
    even, top = is_even("lat"), is_top()

    @pl.when(even)
    def _():
        unpack_south(far, raw, x, lev)
        unpack_north(near, raw, x, lev)

    @pl.when(jnp.logical_not(even))
    def _():
        unpack_south(near, raw, x, lev)

        @pl.when(top)
        def _():
            unpack_fold(far, flat, raw, x, lev)

        @pl.when(jnp.logical_not(top))
        def _():
            unpack_north(far, raw, x, lev)
    pack_sides(
        (0, 3), None, None, raw, x, lambda tile: lev[plain(tile // 3), :],
        near_side, far_side, packed_all,
    )


def tile_of(own, beside, where, tile):
    i, k = where
    if tile in (1, 2):
        return own[i][k, plain(tile - 1), :] if isinstance(own, tuple) else own[i, k, plain(tile - 1), :]
    return beside[i, k, plain(tile // 3), :]


def run_steps(x, xb, doms, raw, table, derived, seam_derived, work):
    dz, tz, fx, fy, tx, ty, fseam = work
    derive(raw, derived, seam_derived, table)
    now, later = x, xb
    for step in range(STEPS):
        tiles = (1, 2) if step == STEPS - 1 else (0, 1, 2, 3)
        grads_pass(now, doms, table, dz, tz)
        sides_pass(now, doms, table, derived, seam_derived, tz, fx, fy, tx, ty, fseam, tiles)
        sum_pass(now, later, doms, table, derived, dz, fx, fy, tx, ty, fseam, tiles)
        now, later = later, now
    return now


def level_of(levels, beside, tile):
    if tile in (1, 2):
        return levels[plain(tile - 1), :].astype(jnp.float32)
    return beside[plain(tile // 3), :]


def shift_fold(raw):
    @pl.when(jnp.logical_not(is_top()))
    def _():
        for f in NORTHWARD:
            for k in range(K):
                raw[f, k, 31:32, :] = raw[f, k, 23:24, :]

    @pl.when(is_top())
    def _():
        for f in EASTWARD:
            for k in range(K):
                raw[f, k, 24:32, :] = lane_roll(raw[f, k, 24:32, :], -1)


def main_kernel(tracers, levels, *refs):
    statics = refs[:STATICS]
    beside, x_beside, lev, out, raw, x, xb, table, derived, seam_derived = refs[STATICS : STATICS + 10]
    for tile in range(4):
        for k in range(K):
            for f in range(STATICS):
                raw[f, k, plain(tile), :] = tile_of(statics, beside, (f, k), tile)
            for t in range(2):
                x[t, k, at(tile), :] = tile_of(tracers, x_beside, (t, k), tile)
    shift_fold(raw)
    level = jnp.concatenate([level_of(levels, lev, tile) for tile in range(4)], axis=0)
    level_tables(level, table)
    now = run_steps(x, xb, (0, 1), raw, table, derived, seam_derived, refs[STATICS + 10 :])
    for t in range(2):
        for k in range(K):
            out[t, k] = now[t, k, 16:32, :]


def strip_kernel(tracers, levels, *refs):
    statics = refs[:STATICS]
    beside, x_beside, lev, near_own, far_own, near_side, far_side, middle, out = refs[STATICS : STATICS + 9]
    raw, x, xb, table, derived, seam_derived, halo, slev, second = refs[STATICS + 9 : STATICS + 18]
    even_lon = is_even("lon")
    for tile in range(4):
        for u in range(HALVES):
            a, b = (near_own, far_own) if tile in (1, 2) else (near_side, far_side)
            at_tile = (0, 0, 1, 1)[tile]
            expand(halo, tile, u, a[at_tile, u], b[at_tile, u], even_lon)

    lane8 = lanes_of((8, LANES))
    half = lane8 % 64
    in_halo = (half >= 24) & (half < 40)
    low, first = half < 24, lane8 < 64

    def strip(own, tile, slot):
        both = jnp.where(low, lane_roll(own, 24), lane_roll(own, 40))
        packed = halo[tile, slot // 8]
        return jnp.where(in_halo, lane_roll(packed, 24 - 16 * (slot % 8)), both)

    def twice(strip64):
        return jnp.where(first, strip64, lane_roll(strip64, 64))

    for tile in range(4):
        rows = plain(tile)
        for f in range(STATICS):
            for k in range(K):
                own = tile_of(statics, beside, (f, k), tile)
                raw[f, k, rows, :] = strip(own, tile, f * K + k)
        for k in range(K):
            own = [tile_of(tracers, x_beside, (t, k), tile) for t in range(2)]
            x[0, k, at(tile), :] = strip(own[0], tile, 120 + k)
            second[k, rows, :] = strip(own[1], tile, 132 + k)
        slev[rows, :] = twice(strip(level_of(levels, lev, tile), tile, 144))
    for tile in range(4):
        rows = plain(tile)
        for f in range(STATICS):
            for k in range(K):
                raw[f, k, rows, :] = twice(raw[f, k, rows, :])
        for k in range(K):
            x[0, k, at(tile), :] = jnp.where(
                first, x[0, k, at(tile), :], lane_roll(second[k, rows, :], 64)
            )
    shift_fold(raw)
    level_tables(slev[...], table)
    now = run_steps(x, xb, (0,), raw, table, derived, seam_derived, refs[STATICS + 18 :])
    for t in range(2):
        for k in range(K):
            for tile in (1, 2):
                s = now[0, k, at(tile), :]
                west, east = lane_roll(s, -40 - 64 * t), lane_roll(s, 104 - 64 * t)
                rows = plain(tile - 1)
                out[t, k, rows, :] = jnp.where(
                    lane8 < 6, west, jnp.where(lane8 >= 122, east, middle[t, k, rows, :])
                )


def swaps(count, first, wrap):
    pairs = []
    for low in range(first, count if wrap else count - 1, 2):
        high = (low + 1) % count
        pairs += [(low, high), (high, low)]
    return pairs


def swap(array, lat, lon):
    bands, count = lax.axis_size("lat"), lax.axis_size("lon")
    if lat is None:
        return lax.ppermute(array, "lon", swaps(count, lon, True))
    columns = list(range(count))
    if lon is not None:
        for low, high in swaps(count, lon, True):
            columns[low] = high
    pairs = [
        (low * count + i, high * count + columns[i])
        for low, high in swaps(bands, lat, False)
        for i in range(count)
    ]
    if lat == 1:
        last = (bands - 1) * count
        pairs += [(last + i, last + count - 1 - columns[i]) for i in range(count)]
    return lax.ppermute(array, ("lat", "lon"), pairs)


def shape(*dims):
    return jax.ShapeDtypeStruct(dims, jnp.float32)


def params(limit=VMEM_LIMIT):
    return pltpu.CompilerParams(vmem_limit_bytes=limit)


def body(tracers, wet_levels, ce, cn, cd, de, se, dn, sn, dd, dse, dsn):
    statics = (ce, de, se, cn, dn, sn, cd, dd, dse, dsn)
    band, side, own = shape(BAND * K, LANES), shape(2, HALVES, 8, LANES), shape(2, HALVES, 8, LANES)
    near, far, near_own, far_own = pl.pallas_call(
        pack_kernel,
        out_shape=(band, band, own, own),
        scratch_shapes=vmem((2, SLOTS + 1, 8, LANES)),
        compiler_params=params(FULL),
        name="pack",
    )(tracers, wet_levels, *statics)
    far = swap(far, 1, None)
    near = swap(near, 0, None)
    near_own = swap(near_own, None, 0)
    far_own = swap(far_own, None, 1)
    beside, x_beside, lev, near_side, far_side = pl.pallas_call(
        middle_kernel,
        out_shape=(
            shape(STATICS, K, 16, LANES), shape(2, K, 16, LANES), shape(16, LANES), side, side,
        ),
        scratch_shapes=vmem((K, BAND, LANES), (2, SLOTS + 1, 8, LANES)),
        compiler_params=params(),
        name="middle",
    )(near, far)
    far_side = swap(far_side, None, 1)
    near_side = swap(near_side, None, 0)
    inner = pl.pallas_call(
        main_kernel,
        out_shape=shape(2, K, ROWS, LANES),
        scratch_shapes=step_scratch(2),
        compiler_params=params(),
        cost_estimate=pl.CostEstimate(flops=20_000_000, bytes_accessed=20_000_000, transcendentals=0),
        name="blocks",
    )(tracers, wet_levels, *statics, beside, x_beside, lev)
    return pl.pallas_call(
        strip_kernel,
        out_shape=shape(2, K, ROWS, LANES),
        scratch_shapes=step_scratch(1, (4, SLOTS + 1, 8, LANES), (EXT, LANES), (K, EXT, LANES)),
        compiler_params=params(),
        name="strips",
    )(
        tracers, wet_levels, *statics, beside, x_beside, lev,
        near_own, far_own, near_side, far_side, inner,
    )


def vmem(*all_dims):
    return [pltpu.VMEM(dims, jnp.float32) for dims in all_dims]


def step_scratch(doms, *more):
    flat, padded = (doms, K, EXT, LANES), (doms, K, PAD, LANES)
    return vmem(
        (STATICS, K, EXT, LANES), padded, padded, (3, PAD, LANES),
        (13, K, EXT, LANES), (4, K, 8, LANES), *more,
        flat, padded, flat, padded, flat, flat, (doms, K, 8, LANES),
    )


def solution(mesh):
    field = P(None, "lat", "lon")
    whole = P(None, None, "lat", "lon")
    in_specs = (whole, P("lat", "lon")) + (field,) * STATICS
    return jax.shard_map(body, mesh=mesh, in_specs=in_specs, out_specs=whole, check_vma=False)
```

time: 50.9 us -> 47 us (0.923)
  the two profiles are of different devices: /device:TPU:14 before, /device:TPU:6 now
where the time goes in v1:
time: 47 us; the launch traced here: 46.8 us
  starting transfers between devices  21.6 us (46%)
  waiting for transfers between devices  12.6 us (27%)
  Pallas kernels  12.3 us (26%)
    ppermute x4, starting transfers between devices, swap(): return lax.ppermute(array, 'lon', swaps(count, lon, True))  17.4 us
    ppermute x2, waiting for transfers between devices, swap(): return lax.ppermute(array, ('lat', 'lon'), pairs)  12.6 us
    pallas_call x1, Pallas kernels, body(): pl.pallas_call(strip_kernel, out_shape=shape(2, K, ROWS, LANES), scratch_...  5.44 us
    ppermute x2, starting transfers between devices, swap(): return lax.ppermute(array, ('lat', 'lon'), pairs)  4.19 us
    pallas_call x1, Pallas kernels, body(): pl.pallas_call(main_kernel, out_shape=shape(2, K, ROWS, LANES), scratch_s...  3.5 us
    pallas_call x1, Pallas kernels, body(): pl.pallas_call(pack_kernel, out_shape=(band, band, own, own), scratch_sha...  2.71 us
  transfers between devices with their start and end apart: 6, of which 1 were waited for; matrix products, arithmetic and copies ran while one was open for 0% of the time, Pallas kernels for 9%

profile of v1, /device:TPU:6, one launch (start us, length us, event | category | flops | bytes accessed | tf_op | source)
XLA Modules:
  0.0 46.8 jit_solution(4817693030592478669)
XLA Ops:
  0.0 0.0 copy-start.6
  0.0 0.0 copy-start.7
  0.0 0.0 copy-start.8
  0.0 0.0 copy-start.9
  0.0 0.0 copy-start.10
  0.0 2.7 %pack.1 = (f32[672,128]{1,0:T(8,128)}, f32[672,128]{1,0:T(8,128)}, f32[2,10,8,128]{3,2,1,0:T(8,128)}, f32[2,10,8,128]{3,2,1,0:T(8,128)}) custom-call(f32[2,12,16,128]{3,2,1,0:T(8,128)} %tracers.5, s32[16,128]{1,0:T(8,128)} %levels.5, f32[12,16,128]{2,1,0:T(8,128)} %refs_0_.5, f32[12,16,128]{2,1,0:T(8,128)} %refs_1_.5, f32[12,16,128]{2,1,0:T(8,128)} %refs_2_.5, ...), custom_call_target="tpu_custom_call" | custom-call | tf_op jit(solution)/shard_map/pack/pallas_call | solution.py:499
  2.7 1.6 %collective-permute-start = (f32[672,128]{1,0:T(8,128)}, f32[672,128]{1,0:T(8,128)S(1)}, u32[]{:S(2)}, u32[]{:S(2)}) collective-permute-start(f32[672,128]{1,0:T(8,128)} %get-tuple-element.14), channel_id=1, source_target_pairs={{0,32},{1,33},{2,34},{3,35},{4,36},{5,37},{6,38},{7,39},{8,40},{9,... | collective-permute-start | bytes 1032200 | tf_op jit(solution)/shard_map/ppermute | solution.py:485
  4.3 2.6 %collective-permute-start.1 = (f32[672,128]{1,0:T(8,128)}, f32[672,128]{1,0:T(8,128)S(1)}, u32[]{:S(2)}, u32[]{:S(2)}) collective-permute-start(f32[672,128]{1,0:T(8,128)} %get-tuple-element.15), channel_id=1, source_target_pairs={{32,64},{33,65},{34,66},{35,67},{36,68},{37,69},{38,70},{39,71},{4... | collective-permute-start | bytes 1032200 | tf_op jit(solution)/shard_map/ppermute | solution.py:485
  6.9 0.1 collective-permute-start.2
  7.0 0.0 copy-start
  7.0 0.0 copy-start.1
  7.1 0.0 copy-start.2
  7.1 0.0 copy-start.3
  7.1 0.0 copy-start.4
  7.1 0.0 copy-start.5
  7.1 8.6 %collective-permute-start.3 = (f32[2,10,8,128]{3,2,1,0:T(8,128)}, f32[2,10,8,128]{3,2,1,0:T(8,128)S(1)}, u32[]{:S(2)}, u32[]{:S(2)}) collective-permute-start(f32[2,10,8,128]{3,2,1,0:T(8,128)} %get-tuple-element.20), channel_id=1, source_target_pairs={{1,2},{2,1},{3,4},{4,3},{5,6},{6,5},{7,8},{8,7},{9,10},{10,9},{11,... | collective-permute-start | bytes 245768 | tf_op jit(solution)/shard_map/ppermute | solution.py:472
  15.7 12.6 %collective-permute-done.near = f32[672,128]{1,0:T(8,128)S(1)} collective-permute-done((f32[672,128]{1,0:T(8,128)}, f32[672,128]{1,0:T(8,128)S(1)}, u32[]{:S(2)}, u32[]{:S(2)}) %collective-permute-start) | collective-permute-done | bytes 344096 | tf_op jit(solution)/shard_map/ppermute | solution.py:485
  28.4 0.0 collective-permute-done.1.far
  28.4 0.7 %middle.1 = (f32[10,12,16,128]{3,2,1,0:T(8,128)S(1)}, f32[2,12,16,128]{3,2,1,0:T(8,128)S(1)}, f32[16,128]{1,0:T(8,128)S(1)}, f32[2,10,8,128]{3,2,1,0:T(8,128)S(1)}, f32[2,10,8,128]{3,2,1,0:T(8,128)S(1)}) custom-call(f32[672,128]{1,0:T(8,128)S(1)} %collective-permute-done.near, f32[672,128]{1,0:T(8,128)S(1)} %collective-permute-done.1.far), custom_call_target="tpu_custom_call" | custom-call | tf_op jit(solution)/shard_map/middle/pallas_call | solution.py:510
  29.1 0.0 copy-start.11
  29.1 0.1 collective-permute-start.4
  29.2 8.6 %collective-permute-start.5 = (f32[2,10,8,128]{3,2,1,0:T(8,128)S(1)}, f32[2,10,8,128]{3,2,1,0:T(8,128)S(1)}, u32[]{:S(2)}, u32[]{:S(2)}) collective-permute-start(f32[2,10,8,128]{3,2,1,0:T(8,128)S(1)} %get-tuple-element.22), channel_id=1, source_target_pairs={{1,2},{2,1},{3,4},{4,3},{5,6},{6,5},{7,8},{8,7},{9,10},{10,9},{11,... | collective-permute-start | bytes 245768 | tf_op jit(solution)/shard_map/ppermute | solution.py:472
  37.8 0.0 copy-done.6
  37.8 0.0 copy-done.7
  37.8 0.0 copy-done.8
  37.8 0.0 copy-done.9
  37.8 0.0 copy-done.10
  37.8 0.0 copy-done
  37.8 0.0 copy-done.1
  37.8 0.0 copy-done.2
  37.8 0.0 copy-done.3
  37.8 0.0 copy-done.4
  37.8 0.0 copy-done.5
  37.8 0.0 copy-done.11
  37.8 3.5 %blocks.1.refs_17_ = f32[2,12,16,128]{3,2,1,0:T(8,128)S(1)} custom-call(f32[2,12,16,128]{3,2,1,0:T(8,128)S(1)} %copy-done, s32[16,128]{1,0:T(8,128)S(1)} %copy-done.11, f32[12,16,128]{2,1,0:T(8,128)S(1)} %copy-done.1, f32[12,16,128]{2,1,0:T(8,128)S(1)} %copy-done.2, f32[12,16,128]{2,1,0:T(8,128)S(1)} %copy-done.3, f32[12,16,128]{2,1,0:T(8,128)S(1)} %copy-done.4, ...), custom_call_target="tpu_custom_call" | custom-call | flops 20000000 | bytes 20000000 | tf_op jit(solution)/shard_map/blocks/pallas_call | solution.py:521
  41.4 0.0 collective-permute-done.2.refs_13_
  41.4 0.0 collective-permute-done.3.refs_14_
  41.4 0.0 collective-permute-done.4.refs_15_
  41.4 0.0 collective-permute-done.5.refs_16_
  41.4 5.4 %strips.1 = f32[2,12,16,128]{3,2,1,0:T(8,128)} custom-call(f32[2,12,16,128]{3,2,1,0:T(8,128)S(1)} %copy-done, s32[16,128]{1,0:T(8,128)S(1)} %copy-done.11, f32[12,16,128]{2,1,0:T(8,128)S(1)} %copy-done.1, f32[12,16,128]{2,1,0:T(8,128)S(1)} %copy-done.2, f32[12,16,128]{2,1,0:T(8,128)S(1)} %copy-done.3, f32[12,16,128]{2,1,0:T(8,128)S(1)} %copy-done.4, ...), custom_call_target="tpu_custom_call" | custom-call | tf_op jit(solution)/shard_map/strips/pallas_call | solution.py:529
Async XLA Ops:
  0.0 37.8 %copy-start.6 = (f32[12,16,128]{2,1,0:T(8,128)S(1)}, f32[12,16,128]{2,1,0:T(8,128)}, u32[]{:S(2)}) copy-start(f32[12,16,128]{2,1,0:T(8,128)} %refs_5_.5) | copy-start | bytes 294916
  0.0 37.8 %copy-start.7 = (f32[12,16,128]{2,1,0:T(8,128)S(1)}, f32[12,16,128]{2,1,0:T(8,128)}, u32[]{:S(2)}) copy-start(f32[12,16,128]{2,1,0:T(8,128)} %refs_6_.5) | copy-start | bytes 294916
  0.0 37.8 %copy-start.8 = (f32[12,16,128]{2,1,0:T(8,128)S(1)}, f32[12,16,128]{2,1,0:T(8,128)}, u32[]{:S(2)}) copy-start(f32[12,16,128]{2,1,0:T(8,128)} %refs_7_.5) | copy-start | bytes 294916
  0.0 37.8 %copy-start.9 = (f32[12,16,128]{2,1,0:T(8,128)S(1)}, f32[12,16,128]{2,1,0:T(8,128)}, u32[]{:S(2)}) copy-start(f32[12,16,128]{2,1,0:T(8,128)} %refs_8_.5) | copy-start | bytes 294916
  0.0 37.8 %copy-start.10 = (f32[12,16,128]{2,1,0:T(8,128)S(1)}, f32[12,16,128]{2,1,0:T(8,128)}, u32[]{:S(2)}) copy-start(f32[12,16,128]{2,1,0:T(8,128)} %refs_9_.5) | copy-start | bytes 294916
  2.7 25.6 %collective-permute-start = (f32[672,128]{1,0:T(8,128)}, f32[672,128]{1,0:T(8,128)S(1)}, u32[]{:S(2)}, u32[]{:S(2)}) collective-permute-start(f32[672,128]{1,0:T(8,128)} %get-tuple-element.14), channel_id=1, source_target_pairs={{0,32},{1,33},{2,34},{3,35},{4,36},{5,37},{6,38},{7,39},{8,40},{9,... | collective-permute-start | bytes 1032200 | tf_op jit(solution)/shard_map/ppermute | solution.py:485
  4.3 24.1 %collective-permute-start.1 = (f32[672,128]{1,0:T(8,128)}, f32[672,128]{1,0:T(8,128)S(1)}, u32[]{:S(2)}, u32[]{:S(2)}) collective-permute-start(f32[672,128]{1,0:T(8,128)} %get-tuple-element.15), channel_id=1, source_target_pairs={{32,64},{33,65},{34,66},{35,67},{36,68},{37,69},{38,70},{39,71},{4... | collective-permute-start | bytes 1032200 | tf_op jit(solution)/shard_map/ppermute | solution.py:485
  6.9 34.4 %collective-permute-start.2 = (f32[2,10,8,128]{3,2,1,0:T(8,128)}, f32[2,10,8,128]{3,2,1,0:T(8,128)S(1)}, u32[]{:S(2)}, u32[]{:S(2)}) collective-permute-start(f32[2,10,8,128]{3,2,1,0:T(8,128)} %get-tuple-element.19), channel_id=1, source_target_pairs={{0,1},{1,0},{2,3},{3,2},{4,5},{5,4},{6,7},{7,6},{8,9},{9,8},{10,11... | collective-permute-start | bytes 245768 | tf_op jit(solution)/shard_map/ppermute | solution.py:472
  7.0 30.7 %copy-start = (f32[2,12,16,128]{3,2,1,0:T(8,128)S(1)}, f32[2,12,16,128]{3,2,1,0:T(8,128)}, u32[]{:S(2)}) copy-start(f32[2,12,16,128]{3,2,1,0:T(8,128)} %tracers.5) | copy-start | bytes 589828
  7.0 30.7 %copy-start.1 = (f32[12,16,128]{2,1,0:T(8,128)S(1)}, f32[12,16,128]{2,1,0:T(8,128)}, u32[]{:S(2)}) copy-start(f32[12,16,128]{2,1,0:T(8,128)} %refs_0_.5) | copy-start | bytes 294916
  7.1 30.7 %copy-start.2 = (f32[12,16,128]{2,1,0:T(8,128)S(1)}, f32[12,16,128]{2,1,0:T(8,128)}, u32[]{:S(2)}) copy-start(f32[12,16,128]{2,1,0:T(8,128)} %refs_1_.5) | copy-start | bytes 294916
  7.1 30.7 %copy-start.3 = (f32[12,16,128]{2,1,0:T(8,128)S(1)}, f32[12,16,128]{2,1,0:T(8,128)}, u32[]{:S(2)}) copy-start(f32[12,16,128]{2,1,0:T(8,128)} %refs_2_.5) | copy-start | bytes 294916
  7.1 30.7 %copy-start.4 = (f32[12,16,128]{2,1,0:T(8,128)S(1)}, f32[12,16,128]{2,1,0:T(8,128)}, u32[]{:S(2)}) copy-start(f32[12,16,128]{2,1,0:T(8,128)} %refs_3_.5) | copy-start | bytes 294916
  7.1 30.7 %copy-start.5 = (f32[12,16,128]{2,1,0:T(8,128)S(1)}, f32[12,16,128]{2,1,0:T(8,128)}, u32[]{:S(2)}) copy-start(f32[12,16,128]{2,1,0:T(8,128)} %refs_4_.5) | copy-start | bytes 294916
  7.1 34.3 %collective-permute-start.3 = (f32[2,10,8,128]{3,2,1,0:T(8,128)}, f32[2,10,8,128]{3,2,1,0:T(8,128)S(1)}, u32[]{:S(2)}, u32[]{:S(2)}) collective-permute-start(f32[2,10,8,128]{3,2,1,0:T(8,128)} %get-tuple-element.20), channel_id=1, source_target_pairs={{1,2},{2,1},{3,4},{4,3},{5,6},{6,5},{7,8},{8,7},{9,10},{10,9},{11,... | collective-permute-start | bytes 245768 | tf_op jit(solution)/shard_map/ppermute | solution.py:472
  29.1 8.8 %copy-start.11 = (s32[16,128]{1,0:T(8,128)S(1)}, s32[16,128]{1,0:T(8,128)}, u32[]{:S(2)}) copy-start(s32[16,128]{1,0:T(8,128)} %levels.5) | copy-start | bytes 24580
  29.1 12.3 %collective-permute-start.4 = (f32[2,10,8,128]{3,2,1,0:T(8,128)S(1)}, f32[2,10,8,128]{3,2,1,0:T(8,128)S(1)}, u32[]{:S(2)}, u32[]{:S(2)}) collective-permute-start(f32[2,10,8,128]{3,2,1,0:T(8,128)S(1)} %get-tuple-element.21), channel_id=1, source_target_pairs={{0,1},{1,0},{2,3},{3,2},{4,5},{5,4},{6,7},{7,6},{8,9},{9,8},{10,11... | collective-permute-start | bytes 245768 | tf_op jit(solution)/shard_map/ppermute | solution.py:472
  29.2 12.2 %collective-permute-start.5 = (f32[2,10,8,128]{3,2,1,0:T(8,128)S(1)}, f32[2,10,8,128]{3,2,1,0:T(8,128)S(1)}, u32[]{:S(2)}, u32[]{:S(2)}) collective-permute-start(f32[2,10,8,128]{3,2,1,0:T(8,128)S(1)} %get-tuple-element.22), channel_id=1, source_target_pairs={{1,2},{2,1},{3,4},{4,3},{5,6},{6,5},{7,8},{8,7},{9,10},{10,9},{11,... | collective-permute-start | bytes 245768 | tf_op jit(solution)/shard_map/ppermute | solution.py:472

commit v2 on v1

--- a/solution.py
+++ b/solution.py
@@ -412,14 +412,13 @@
             expand(halo, tile, u, a[at_tile, u], b[at_tile, u], even_lon)
 
     lane8 = lanes_of((8, LANES))
-    half = lane8 % 64
-    in_halo = (half >= 24) & (half < 40)
-    low, first = half < 24, lane8 < 64
+    in_halo, natural = lane8 < 16, lane8 >= 104
+    first = natural | (lane8 < 40)
 
     def strip(own, tile, slot):
-        both = jnp.where(low, lane_roll(own, 24), lane_roll(own, 40))
+        both = jnp.where(natural, own, lane_roll(own, 16))
         packed = halo[tile, slot // 8]
-        return jnp.where(in_halo, lane_roll(packed, 24 - 16 * (slot % 8)), both)
+        return jnp.where(in_halo, lane_roll(packed, -16 * (slot % 8)), both)
 
     def twice(strip64):
         return jnp.where(first, strip64, lane_roll(strip64, 64))
@@ -451,7 +450,7 @@
         for k in range(K):
             for tile in (1, 2):
                 s = now[0, k, at(tile), :]
-                west, east = lane_roll(s, -40 - 64 * t), lane_roll(s, 104 - 64 * t)
+                west, east = lane_roll(s, -16 - 64 * t), lane_roll(s, 64) if t else s
                 rows = plain(tile - 1)
                 out[t, k, rows, :] = jnp.where(
                     lane8 < 6, west, jnp.where(lane8 >= 122, east, middle[t, k, rows, :])

time: 47 us -> 46.1 us (0.981)
  Pallas kernels: 12.3 us -> 11.4 us
    pallas_call x1, Pallas kernels: 5.44 us -> 4.54 us  [body(): pl.pallas_call(strip_kernel, out_shape=shape(2, K, ROWS, LANES), scratch_...]
where the time goes in v2:
time: 46.1 us; the launch traced here: 45.9 us
  starting transfers between devices  21.6 us (47%)
  waiting for transfers between devices  12.6 us (27%)
  Pallas kernels  11.4 us (25%)
    ppermute x4, starting transfers between devices, swap(): return lax.ppermute(array, 'lon', swaps(count, lon, True))  17.4 us
    ppermute x2, waiting for transfers between devices, swap(): return lax.ppermute(array, ('lat', 'lon'), pairs)  12.6 us
    pallas_call x1, Pallas kernels, body(): pl.pallas_call(strip_kernel, out_shape=shape(2, K, ROWS, LANES), scratch_...  4.54 us
    ppermute x2, starting transfers between devices, swap(): return lax.ppermute(array, ('lat', 'lon'), pairs)  4.19 us
    pallas_call x1, Pallas kernels, body(): pl.pallas_call(main_kernel, out_shape=shape(2, K, ROWS, LANES), scratch_s...  3.5 us
    pallas_call x1, Pallas kernels, body(): pl.pallas_call(pack_kernel, out_shape=(band, band, own, own), scratch_sha...  2.71 us
  transfers between devices with their start and end apart: 6, of which 1 were waited for; matrix products, arithmetic and copies ran while one was open for 0% of the time, Pallas kernels for 9%

profile of v2, /device:TPU:6, one launch (start us, length us, event | category | flops | bytes accessed | tf_op | source)
XLA Modules:
  0.0 45.9 jit_solution(17278577180893774044)
XLA Ops:
  0.0 0.0 copy-start.6
  0.0 0.0 copy-start.7
  0.0 0.0 copy-start.8
  0.0 0.0 copy-start.9
  0.0 0.0 copy-start.10
  0.0 2.7 %pack.1 = (f32[672,128]{1,0:T(8,128)}, f32[672,128]{1,0:T(8,128)}, f32[2,10,8,128]{3,2,1,0:T(8,128)}, f32[2,10,8,128]{3,2,1,0:T(8,128)}) custom-call(f32[2,12,16,128]{3,2,1,0:T(8,128)} %tracers.5, s32[16,128]{1,0:T(8,128)} %levels.5, f32[12,16,128]{2,1,0:T(8,128)} %refs_0_.5, f32[12,16,128]{2,1,0:T(8,128)} %refs_1_.5, f32[12,16,128]{2,1,0:T(8,128)} %refs_2_.5, ...), custom_call_target="tpu_custom_call" | custom-call | tf_op jit(solution)/shard_map/pack/pallas_call | solution.py:498
  2.7 1.6 %collective-permute-start = (f32[672,128]{1,0:T(8,128)}, f32[672,128]{1,0:T(8,128)S(1)}, u32[]{:S(2)}, u32[]{:S(2)}) collective-permute-start(f32[672,128]{1,0:T(8,128)} %get-tuple-element.14), channel_id=1, source_target_pairs={{0,32},{1,33},{2,34},{3,35},{4,36},{5,37},{6,38},{7,39},{8,40},{9,... | collective-permute-start | bytes 1032200 | tf_op jit(solution)/shard_map/ppermute | solution.py:484
  4.3 2.6 %collective-permute-start.1 = (f32[672,128]{1,0:T(8,128)}, f32[672,128]{1,0:T(8,128)S(1)}, u32[]{:S(2)}, u32[]{:S(2)}) collective-permute-start(f32[672,128]{1,0:T(8,128)} %get-tuple-element.15), channel_id=1, source_target_pairs={{32,64},{33,65},{34,66},{35,67},{36,68},{37,69},{38,70},{39,71},{4... | collective-permute-start | bytes 1032200 | tf_op jit(solution)/shard_map/ppermute | solution.py:484
  6.9 0.1 collective-permute-start.2
  7.0 0.0 copy-start
  7.0 0.0 copy-start.1
  7.1 0.0 copy-start.2
  7.1 0.0 copy-start.3
  7.1 0.0 copy-start.4
  7.1 0.0 copy-start.5
  7.1 8.6 %collective-permute-start.3 = (f32[2,10,8,128]{3,2,1,0:T(8,128)}, f32[2,10,8,128]{3,2,1,0:T(8,128)S(1)}, u32[]{:S(2)}, u32[]{:S(2)}) collective-permute-start(f32[2,10,8,128]{3,2,1,0:T(8,128)} %get-tuple-element.20), channel_id=1, source_target_pairs={{1,2},{2,1},{3,4},{4,3},{5,6},{6,5},{7,8},{8,7},{9,10},{10,9},{11,... | collective-permute-start | bytes 245768 | tf_op jit(solution)/shard_map/ppermute | solution.py:471
  15.7 12.6 %collective-permute-done.near = f32[672,128]{1,0:T(8,128)S(1)} collective-permute-done((f32[672,128]{1,0:T(8,128)}, f32[672,128]{1,0:T(8,128)S(1)}, u32[]{:S(2)}, u32[]{:S(2)}) %collective-permute-start) | collective-permute-done | bytes 344096 | tf_op jit(solution)/shard_map/ppermute | solution.py:484
  28.4 0.0 collective-permute-done.1.far
  28.4 0.7 %middle.1 = (f32[10,12,16,128]{3,2,1,0:T(8,128)S(1)}, f32[2,12,16,128]{3,2,1,0:T(8,128)S(1)}, f32[16,128]{1,0:T(8,128)S(1)}, f32[2,10,8,128]{3,2,1,0:T(8,128)S(1)}, f32[2,10,8,128]{3,2,1,0:T(8,128)S(1)}) custom-call(f32[672,128]{1,0:T(8,128)S(1)} %collective-permute-done.near, f32[672,128]{1,0:T(8,128)S(1)} %collective-permute-done.1.far), custom_call_target="tpu_custom_call" | custom-call | tf_op jit(solution)/shard_map/middle/pallas_call | solution.py:509
  29.1 0.0 copy-start.11
  29.1 0.1 collective-permute-start.4
  29.2 8.6 %collective-permute-start.5 = (f32[2,10,8,128]{3,2,1,0:T(8,128)S(1)}, f32[2,10,8,128]{3,2,1,0:T(8,128)S(1)}, u32[]{:S(2)}, u32[]{:S(2)}) collective-permute-start(f32[2,10,8,128]{3,2,1,0:T(8,128)S(1)} %get-tuple-element.22), channel_id=1, source_target_pairs={{1,2},{2,1},{3,4},{4,3},{5,6},{6,5},{7,8},{8,7},{9,10},{10,9},{11,... | collective-permute-start | bytes 245768 | tf_op jit(solution)/shard_map/ppermute | solution.py:471
  37.8 0.0 copy-done.6
  37.8 0.0 copy-done.7
  37.8 0.0 copy-done.8
  37.8 0.0 copy-done.9
  37.8 0.0 copy-done.10
  37.8 0.0 copy-done
  37.8 0.0 copy-done.1
  37.8 0.0 copy-done.2
  37.8 0.0 copy-done.3
  37.8 0.0 copy-done.4
  37.8 0.0 copy-done.5
  37.8 0.0 copy-done.11
  37.8 3.5 %blocks.1.refs_17_ = f32[2,12,16,128]{3,2,1,0:T(8,128)S(1)} custom-call(f32[2,12,16,128]{3,2,1,0:T(8,128)S(1)} %copy-done, s32[16,128]{1,0:T(8,128)S(1)} %copy-done.11, f32[12,16,128]{2,1,0:T(8,128)S(1)} %copy-done.1, f32[12,16,128]{2,1,0:T(8,128)S(1)} %copy-done.2, f32[12,16,128]{2,1,0:T(8,128)S(1)} %copy-done.3, f32[12,16,128]{2,1,0:T(8,128)S(1)} %copy-done.4, ...), custom_call_target="tpu_custom_call" | custom-call | flops 20000000 | bytes 20000000 | tf_op jit(solution)/shard_map/blocks/pallas_call | solution.py:520
  41.4 0.0 collective-permute-done.2.refs_13_
  41.4 0.0 collective-permute-done.3.refs_14_
  41.4 0.0 collective-permute-done.4.refs_15_
  41.4 0.0 collective-permute-done.5.refs_16_
  41.4 4.5 %strips.1 = f32[2,12,16,128]{3,2,1,0:T(8,128)} custom-call(f32[2,12,16,128]{3,2,1,0:T(8,128)S(1)} %copy-done, s32[16,128]{1,0:T(8,128)S(1)} %copy-done.11, f32[12,16,128]{2,1,0:T(8,128)S(1)} %copy-done.1, f32[12,16,128]{2,1,0:T(8,128)S(1)} %copy-done.2, f32[12,16,128]{2,1,0:T(8,128)S(1)} %copy-done.3, f32[12,16,128]{2,1,0:T(8,128)S(1)} %copy-done.4, ...), custom_call_target="tpu_custom_call" | custom-call | tf_op jit(solution)/shard_map/strips/pallas_call | solution.py:528
Async XLA Ops:
  0.0 37.8 %copy-start.6 = (f32[12,16,128]{2,1,0:T(8,128)S(1)}, f32[12,16,128]{2,1,0:T(8,128)}, u32[]{:S(2)}) copy-start(f32[12,16,128]{2,1,0:T(8,128)} %refs_5_.5) | copy-start | bytes 294916
  0.0 37.8 %copy-start.7 = (f32[12,16,128]{2,1,0:T(8,128)S(1)}, f32[12,16,128]{2,1,0:T(8,128)}, u32[]{:S(2)}) copy-start(f32[12,16,128]{2,1,0:T(8,128)} %refs_6_.5) | copy-start | bytes 294916
  0.0 37.8 %copy-start.8 = (f32[12,16,128]{2,1,0:T(8,128)S(1)}, f32[12,16,128]{2,1,0:T(8,128)}, u32[]{:S(2)}) copy-start(f32[12,16,128]{2,1,0:T(8,128)} %refs_7_.5) | copy-start | bytes 294916
  0.0 37.8 %copy-start.9 = (f32[12,16,128]{2,1,0:T(8,128)S(1)}, f32[12,16,128]{2,1,0:T(8,128)}, u32[]{:S(2)}) copy-start(f32[12,16,128]{2,1,0:T(8,128)} %refs_8_.5) | copy-start | bytes 294916
  0.0 37.8 %copy-start.10 = (f32[12,16,128]{2,1,0:T(8,128)S(1)}, f32[12,16,128]{2,1,0:T(8,128)}, u32[]{:S(2)}) copy-start(f32[12,16,128]{2,1,0:T(8,128)} %refs_9_.5) | copy-start | bytes 294916
  2.7 25.6 %collective-permute-start = (f32[672,128]{1,0:T(8,128)}, f32[672,128]{1,0:T(8,128)S(1)}, u32[]{:S(2)}, u32[]{:S(2)}) collective-permute-start(f32[672,128]{1,0:T(8,128)} %get-tuple-element.14), channel_id=1, source_target_pairs={{0,32},{1,33},{2,34},{3,35},{4,36},{5,37},{6,38},{7,39},{8,40},{9,... | collective-permute-start | bytes 1032200 | tf_op jit(solution)/shard_map/ppermute | solution.py:484
  4.3 24.1 %collective-permute-start.1 = (f32[672,128]{1,0:T(8,128)}, f32[672,128]{1,0:T(8,128)S(1)}, u32[]{:S(2)}, u32[]{:S(2)}) collective-permute-start(f32[672,128]{1,0:T(8,128)} %get-tuple-element.15), channel_id=1, source_target_pairs={{32,64},{33,65},{34,66},{35,67},{36,68},{37,69},{38,70},{39,71},{4... | collective-permute-start | bytes 1032200 | tf_op jit(solution)/shard_map/ppermute | solution.py:484
  6.9 34.4 %collective-permute-start.2 = (f32[2,10,8,128]{3,2,1,0:T(8,128)}, f32[2,10,8,128]{3,2,1,0:T(8,128)S(1)}, u32[]{:S(2)}, u32[]{:S(2)}) collective-permute-start(f32[2,10,8,128]{3,2,1,0:T(8,128)} %get-tuple-element.19), channel_id=1, source_target_pairs={{0,1},{1,0},{2,3},{3,2},{4,5},{5,4},{6,7},{7,6},{8,9},{9,8},{10,11... | collective-permute-start | bytes 245768 | tf_op jit(solution)/shard_map/ppermute | solution.py:471
  7.0 30.7 %copy-start = (f32[2,12,16,128]{3,2,1,0:T(8,128)S(1)}, f32[2,12,16,128]{3,2,1,0:T(8,128)}, u32[]{:S(2)}) copy-start(f32[2,12,16,128]{3,2,1,0:T(8,128)} %tracers.5) | copy-start | bytes 589828
  7.0 30.7 %copy-start.1 = (f32[12,16,128]{2,1,0:T(8,128)S(1)}, f32[12,16,128]{2,1,0:T(8,128)}, u32[]{:S(2)}) copy-start(f32[12,16,128]{2,1,0:T(8,128)} %refs_0_.5) | copy-start | bytes 294916
  7.1 30.7 %copy-start.2 = (f32[12,16,128]{2,1,0:T(8,128)S(1)}, f32[12,16,128]{2,1,0:T(8,128)}, u32[]{:S(2)}) copy-start(f32[12,16,128]{2,1,0:T(8,128)} %refs_1_.5) | copy-start | bytes 294916
  7.1 30.7 %copy-start.3 = (f32[12,16,128]{2,1,0:T(8,128)S(1)}, f32[12,16,128]{2,1,0:T(8,128)}, u32[]{:S(2)}) copy-start(f32[12,16,128]{2,1,0:T(8,128)} %refs_2_.5) | copy-start | bytes 294916
  7.1 30.7 %copy-start.4 = (f32[12,16,128]{2,1,0:T(8,128)S(1)}, f32[12,16,128]{2,1,0:T(8,128)}, u32[]{:S(2)}) copy-start(f32[12,16,128]{2,1,0:T(8,128)} %refs_3_.5) | copy-start | bytes 294916
  7.1 30.7 %copy-start.5 = (f32[12,16,128]{2,1,0:T(8,128)S(1)}, f32[12,16,128]{2,1,0:T(8,128)}, u32[]{:S(2)}) copy-start(f32[12,16,128]{2,1,0:T(8,128)} %refs_4_.5) | copy-start | bytes 294916
  7.1 34.3 %collective-permute-start.3 = (f32[2,10,8,128]{3,2,1,0:T(8,128)}, f32[2,10,8,128]{3,2,1,0:T(8,128)S(1)}, u32[]{:S(2)}, u32[]{:S(2)}) collective-permute-start(f32[2,10,8,128]{3,2,1,0:T(8,128)} %get-tuple-element.20), channel_id=1, source_target_pairs={{1,2},{2,1},{3,4},{4,3},{5,6},{6,5},{7,8},{8,7},{9,10},{10,9},{11,... | collective-permute-start | bytes 245768 | tf_op jit(solution)/shard_map/ppermute | solution.py:471
  29.1 8.8 %copy-start.11 = (s32[16,128]{1,0:T(8,128)S(1)}, s32[16,128]{1,0:T(8,128)}, u32[]{:S(2)}) copy-start(s32[16,128]{1,0:T(8,128)} %levels.5) | copy-start | bytes 24580
  29.1 12.3 %collective-permute-start.4 = (f32[2,10,8,128]{3,2,1,0:T(8,128)S(1)}, f32[2,10,8,128]{3,2,1,0:T(8,128)S(1)}, u32[]{:S(2)}, u32[]{:S(2)}) collective-permute-start(f32[2,10,8,128]{3,2,1,0:T(8,128)S(1)} %get-tuple-element.21), channel_id=1, source_target_pairs={{0,1},{1,0},{2,3},{3,2},{4,5},{5,4},{6,7},{7,6},{8,9},{9,8},{10,11... | collective-permute-start | bytes 245768 | tf_op jit(solution)/shard_map/ppermute | solution.py:471
  29.2 12.2 %collective-permute-start.5 = (f32[2,10,8,128]{3,2,1,0:T(8,128)S(1)}, f32[2,10,8,128]{3,2,1,0:T(8,128)S(1)}, u32[]{:S(2)}, u32[]{:S(2)}) collective-permute-start(f32[2,10,8,128]{3,2,1,0:T(8,128)S(1)} %get-tuple-element.22), channel_id=1, source_target_pairs={{1,2},{2,1},{3,4},{4,3},{5,6},{6,5},{7,8},{8,7},{9,10},{10,9},{11,... | collective-permute-start | bytes 245768 | tf_op jit(solution)/shard_map/ppermute | solution.py:471
